TPU v7x, 256 devices: a whole 4x4x8 slice. The times are simulated.
256 devices in a mesh: tri: 256 (over y, x, z, core).
Axes of the slice: x: 4, y: 4, z: 8, core: 2. Of those that a mesh axis runs over, the one named last changes fastest.
Arguments:
- matrix_tiles: bfloat16 [4096, 12, 128, 128], P('tri'), may hold values from -0.109375 to 0.109375
- columns: int32 [4096, 12], P('tri'), may hold values from 0 to 4095, as said below
- vectors: bfloat16 [16, 524288], P(None, 'tri'), may hold values from -6 to 6
- center: float32 [1], replicated, may hold values from -1 to 1
- halfwidth: float32 [1], replicated, may hold values from 1.5 to 3
Outputs:
- filtered_one: float32 [16, 524288], P(None, 'tri')
- filtered_two: float32 [16, 524288], P(None, 'tri')
Inputs may be any that keep to these rules, and one draw needn't show every extreme that they name: For block row i, columns[i, k] lies between max(0, (i // 16 - 4) * 16) and i; columns[i, 0] = i and columns[i, 1] = max(0, (i // 16 - 4) * 16); entries may repeat, and repeated tiles add.
All inputs are finite; a program needn't handle non-finite values.
Results may differ from a plain program's by a relative error of at most 0.0018.
Values may be sent and summed in bfloat16 or wider, within the bound.
A program may use at most 64 MiB of HBM per device.

v0:
```python
import jax
import jax.numpy as jnp
from jax import lax
from jax.sharding import PartitionSpec as P

SPAN = 4


def passed_along(block, axis, distance):
    devices = range(lax.axis_size(axis))
    route = [(i - distance, i) for i in devices if i - distance in devices]
    return lax.ppermute(block, axis, route)


def fetch_window(blocks):
    pieces = []
    for offset in range(SPAN, 0, -1):
        pieces.append(passed_along(blocks, "tri", offset))
    pieces.append(blocks)
    return jnp.concatenate(pieces, axis=0)


def return_parts(spread, rows_blk):
    parts = [
        spread[(SPAN - offset) * rows_blk : (SPAN - offset + 1) * rows_blk]
        for offset in range(SPAN + 1)
    ]
    received = jnp.zeros_like(parts[0])
    for offset in range(1, SPAN + 1):
        received = received + passed_along(parts[offset], "tri", -offset)
    return parts[0] + received


def per_device(matrix_tiles, columns, vectors, center, halfwidth):
    rows_blk = matrix_tiles.shape[0]
    width = matrix_tiles.shape[2]
    count_vec = vectors.shape[0]
    lowest = (lax.axis_index("tri") - SPAN) * rows_blk
    slot_of = columns - lowest
    row_ids = lowest + SPAN * rows_blk + jnp.arange(rows_blk, dtype=jnp.int32)
    weight = jnp.where(columns == row_ids[:, None], 0.5, 1.0).astype(jnp.float32)
    slot_count = (SPAN + 1) * rows_blk
    flat_slots = slot_of.reshape(-1)

    def apply_local(blocks):
        window = fetch_window(blocks)
        picked = jnp.take(window, flat_slots, axis=0).reshape(rows_blk, -1, count_vec, width)
        forward = jnp.einsum(
            "rkvc,rkac->rkva", picked, matrix_tiles, preferred_element_type=jnp.float32
        )
        forward = jnp.sum(forward * weight[:, :, None, None], axis=1)
        behind = jnp.einsum(
            "rva,rkac->rkvc", blocks, matrix_tiles, preferred_element_type=jnp.float32
        )
        behind = (behind * weight[:, :, None, None]).reshape(-1, count_vec * width)
        spread = jnp.zeros((slot_count, count_vec * width), jnp.float32).at[flat_slots].add(behind)
        spread = spread.reshape(slot_count, count_vec, width)
        return forward + return_parts(spread, rows_blk)

    blocks = vectors.reshape(count_vec, rows_blk, width).transpose(1, 0, 2)
    initial = blocks.astype(jnp.float32)
    first = (apply_local(blocks) - center[0] * initial) / halfwidth[0]
    rounded = first.astype(jnp.bfloat16)
    second = 2.0 * (apply_local(rounded) - center[0] * first) / halfwidth[0] - initial
    first_out = first.transpose(1, 0, 2).reshape(count_vec, rows_blk * width)
    second_out = second.transpose(1, 0, 2).reshape(count_vec, rows_blk * width)
    return (first_out, second_out)


def solution(mesh):
    placed = (P("tri", None, None, None), P("tri", None), P(None, "tri"), P(), P())
    return jax.shard_map(
        per_device,
        mesh=mesh,
        in_specs=placed,
        out_specs=(P(None, "tri"), P(None, "tri")),
        check_vma=False,
    )
```

profile of v0, /device:TPU:25, one launch (start us, length us, event | category | flops | bytes accessed | tf_op | source)
XLA Modules:
  0.0 100.7 jit_solution(17109553077375017504)
XLA Ops:
  0.6 0.8 copy-done
  1.5 4.9 %collective-permute-start = (bf16[16,16,128]{2,1,0:T(8,128)(2,1)S(1)}, bf16[16,16,128]{2,1,0:T(8,128)(2,1)S(1)}, u32[]{:S(2)}, u32[]{:S(2)}) collective-permute-start(bf16[16,16,128]{2,1,0:T(8,128)(2,1)S(1)} %bitcast_bitcast_fusion.1), channel_id=1, source_target_pairs={{0,4},{1,5},{2,6},{3,7},{4,8},{5,9},{6,10},{7,11},{8,12},{9,13},{1... | collective-permute-start | bytes 196616 | tf_op jit(solution)/shard_map/ppermute | solution.py:12
  6.4 7.0 %collective-permute-start.1 = (bf16[16,16,128]{2,1,0:T(8,128)(2,1)S(1)}, bf16[16,16,128]{2,1,0:T(8,128)(2,1)S(1)}, u32[]{:S(2)}, u32[]{:S(2)}) collective-permute-start(bf16[16,16,128]{2,1,0:T(8,128)(2,1)S(1)} %bitcast_bitcast_fusion.1), channel_id=1, source_target_pairs={{0,3},{1,4},{2,5},{3,6},{4,7},{5,8},{6,9},{7,10},{8,11},{9,12},{10... | collective-permute-start | bytes 196616 | tf_op jit(solution)/shard_map/ppermute | solution.py:12
  13.4 2.6 %collective-permute-start.2 = (bf16[16,16,128]{2,1,0:T(8,128)(2,1)S(1)}, bf16[16,16,128]{2,1,0:T(8,128)(2,1)S(1)}, u32[]{:S(2)}, u32[]{:S(2)}) collective-permute-start(bf16[16,16,128]{2,1,0:T(8,128)(2,1)S(1)} %bitcast_bitcast_fusion.1), channel_id=1, source_target_pairs={{0,2},{1,3},{2,4},{3,5},{4,6},{5,7},{6,8},{7,9},{8,10},{9,11},{10,... | collective-permute-start | bytes 196616 | tf_op jit(solution)/shard_map/ppermute | solution.py:12
  16.0 1.9 %collective-permute-start.3 = (bf16[16,16,128]{2,1,0:T(8,128)(2,1)S(1)}, bf16[16,16,128]{2,1,0:T(8,128)(2,1)S(1)}, u32[]{:S(2)}, u32[]{:S(2)}) collective-permute-start(bf16[16,16,128]{2,1,0:T(8,128)(2,1)S(1)} %bitcast_bitcast_fusion.1), channel_id=1, source_target_pairs={{0,1},{1,2},{2,3},{3,4},{4,5},{5,6},{6,7},{7,8},{8,9},{9,10},{10,1... | collective-permute-start | bytes 196616 | tf_op jit(solution)/shard_map/ppermute | solution.py:12
  17.9 0.7 broadcast_subtract_fusion
  18.7 0.8 compare_select_fusion
  19.5 3.7 %convolution_multiply_fusion = f32[16,12,128,16]{2,3,1,0:T(8,128)S(1)} fusion(bf16[16,12,128,128]{3,2,1,0:T(8,128)(2,1)} %param.7, f32[16,12]{1,0:T(8,128)S(1)} %compare_select_fusion, bf16[16,2048]{1,0:T(8,128)(2,1)S(1)} %copy-done), kind=kOutput, calls=%fused_computation.12 | convolution fusion | flops 101056512 | bytes 7930624 | tf_op jit(solution)/shard_map/rva,rkac->rkvc/dot_general | solution.py:52
  23.2 3.6 %scatter_custom_fusion = f32[80,2048]{1,0:T(8,128)S(1)} fusion(s32[192]{0:T(256)S(1)} %bitcast.143, f32[24,8,16,128]{3,2,1,0:T(8,128)S(1)} %bitcast.136, f32[]{:T(128)} %constant.12.clone.1), kind=kCustom, calls=%fused_computation.7 | custom fusion | flops 393216 | bytes 2228228 | tf_op jit(solution)/shard_map/scatter-add | solution.py:56
  27.6 2.4 %collective-permute-start.4 = (f32[16,16,128]{2,1,0:T(8,128)}, f32[16,16,128]{2,1,0:T(8,128)S(1)}, u32[]{:S(2)}, u32[]{:S(2)}) collective-permute-start(f32[16,16,128]{2,1,0:T(8,128)} %bitcast.29), channel_id=1, source_target_pairs={{1,0},{2,1},{3,2},{4,3},{5,4},{6,5},{7,6},{8,7},{9,8},{10,9},{11,1... | collective-permute-start | bytes 393224 | tf_op jit(solution)/shard_map/ppermute | solution.py:12
  30.8 0.7 copy.19
  31.4 0.7 copy.20
  33.5 6.9 %collective-permute-start.5 = (f32[16,16,128]{2,1,0:T(8,128)}, f32[16,16,128]{2,1,0:T(8,128)}, u32[]{:S(2)}, u32[]{:S(2)}) collective-permute-start(f32[16,16,128]{2,1,0:T(8,128)} %bitcast.31), channel_id=1, source_target_pairs={{2,0},{3,1},{4,2},{5,3},{6,4},{7,5},{8,6},{9,7},{10,8},{11,9},{12,... | collective-permute-start | bytes 393224 | tf_op jit(solution)/shard_map/ppermute | solution.py:12
  40.4 1.9 %collective-permute-start.6 = (f32[16,16,128]{2,1,0:T(8,128)}, f32[16,16,128]{2,1,0:T(8,128)}, u32[]{:S(2)}, u32[]{:S(2)}) collective-permute-start(f32[16,16,128]{2,1,0:T(8,128)} %bitcast.33), channel_id=1, source_target_pairs={{3,0},{4,1},{5,2},{6,3},{7,4},{8,5},{9,6},{10,7},{11,8},{12,9},{13... | collective-permute-start | bytes 393224 | tf_op jit(solution)/shard_map/ppermute | solution.py:12
  42.3 3.8 %collective-permute-start.7 = (f32[16,16,128]{2,1,0:T(8,128)}, f32[16,16,128]{2,1,0:T(8,128)}, u32[]{:S(2)}, u32[]{:S(2)}) collective-permute-start(f32[16,16,128]{2,1,0:T(8,128)} %bitcast.35), channel_id=1, source_target_pairs={{4,0},{5,1},{6,2},{7,3},{8,4},{9,5},{10,6},{11,7},{12,8},{13,9},{1... | collective-permute-start | bytes 393224 | tf_op jit(solution)/shard_map/ppermute | solution.py:12
  46.2 0.8 gather_fusion
  47.3 6.3 %multiply_reduce_fusion.1 = f32[16,16,128]{2,1,0:T(8,128)S(1)} fusion(bf16[16,12,16,128]{3,2,1,0:T(8,128)(2,1)S(1)} %bitcast.138, bf16[16,12,128,128]{3,2,1,0:T(8,128)(2,1)} %param.7, f32[16,12]{1,0:T(8,128)S(1)} %compare_select_fusion), kind=kOutput, calls=%fused_computation.11 | convolution fusion | flops 101416960 | bytes 7209728 | tf_op jit(solution)/shard_map/rkvc,rkac->rkva/dot_general | solution.py:48
  53.7 0.9 collective-permute-done.7
  54.6 1.1 %fusion.18 = (bf16[16,16,128]{2,1,0:T(8,128)(2,1)S(1)}, f32[16,16,128]{2,1,0:T(8,128)S(1)}) fusion(f32[]{:T(128)} %bitcast.131, f32[]{:T(128)} %bitcast.129, f32[16,16,128]{2,1,0:T(8,128)S(1)} %multiply_reduce_fusion.1, f32[16,16,128]{2,1,0:T(8,128)} %collective-permute-done.7, f32[16,16,128]{2,1,0:T(8,128)} %collective-permute-done.6, ...), kind=kLoop, calls=%fused_computation.63 | loop fusion | flops 327680 | bytes 1048584 | tf_op jit(solution)/shard_map/convert_element_type | solution.py:63
  55.7 2.4 %collective-permute-start.8 = (bf16[16,16,128]{2,1,0:T(8,128)(2,1)S(1)}, bf16[16,16,128]{2,1,0:T(8,128)(2,1)S(1)}, u32[]{:S(2)}, u32[]{:S(2)}) collective-permute-start(bf16[16,16,128]{2,1,0:T(8,128)(2,1)S(1)} %get-tuple-element.3), channel_id=1, source_target_pairs={{0,4},{1,5},{2,6},{3,7},{4,8},{5,9},{6,10},{7,11},{8,12},{9,13},{1... | collective-permute-start | bytes 196616 | tf_op jit(solution)/shard_map/ppermute | solution.py:12
  58.2 5.3 %collective-permute-start.9 = (bf16[16,16,128]{2,1,0:T(8,128)(2,1)S(1)}, bf16[16,16,128]{2,1,0:T(8,128)(2,1)S(1)}, u32[]{:S(2)}, u32[]{:S(2)}) collective-permute-start(bf16[16,16,128]{2,1,0:T(8,128)(2,1)S(1)} %get-tuple-element.3), channel_id=1, source_target_pairs={{0,3},{1,4},{2,5},{3,6},{4,7},{5,8},{6,9},{7,10},{8,11},{9,12},{10... | collective-permute-start | bytes 196616 | tf_op jit(solution)/shard_map/ppermute | solution.py:12
  63.5 1.9 %collective-permute-start.10 = (bf16[16,16,128]{2,1,0:T(8,128)(2,1)S(1)}, bf16[16,16,128]{2,1,0:T(8,128)(2,1)S(1)}, u32[]{:S(2)}, u32[]{:S(2)}) collective-permute-start(bf16[16,16,128]{2,1,0:T(8,128)(2,1)S(1)} %get-tuple-element.3), channel_id=1, source_target_pairs={{0,2},{1,3},{2,4},{3,5},{4,6},{5,7},{6,8},{7,9},{8,10},{9,11},{10,... | collective-permute-start | bytes 196616 | tf_op jit(solution)/shard_map/ppermute | solution.py:12
  65.4 2.5 %collective-permute-start.11 = (bf16[16,16,128]{2,1,0:T(8,128)(2,1)S(1)}, bf16[16,16,128]{2,1,0:T(8,128)(2,1)S(1)}, u32[]{:S(2)}, u32[]{:S(2)}) collective-permute-start(bf16[16,16,128]{2,1,0:T(8,128)(2,1)S(1)} %get-tuple-element.3), channel_id=1, source_target_pairs={{0,1},{1,2},{2,3},{3,4},{4,5},{5,6},{6,7},{7,8},{8,9},{9,10},{10,1... | collective-permute-start | bytes 196616 | tf_op jit(solution)/shard_map/ppermute | solution.py:12
  67.9 2.1 %convolution_multiply_fusion.1 = f32[16,16,12,128]{3,1,2,0:T(8,128)} fusion(bf16[16,12,128,128]{3,2,1,0:T(8,128)(2,1)S(1)} %bitcast.134, f32[16,12]{1,0:T(8,128)S(1)} %compare_select_fusion, bf16[16,16,128]{2,1,0:T(8,128)(2,1)S(1)} %get-tuple-element.3), kind=kOutput, calls=%fused_computation.13 | convolution fusion | flops 101056512 | bytes 7930624 | tf_op jit(solution)/shard_map/rva,rkac->rkvc/dot_general | solution.py:52
  70.0 4.5 %scatter_custom_fusion.1 = f32[80,2048]{1,0:T(8,128)S(1)} fusion(s32[192]{0:T(256)} %bitcast.144, f32[24,8,16,128]{3,2,1,0:T(8,128)} %bitcast.135, f32[]{:T(128)} %constant.12.clone.1), kind=kCustom, calls=%fused_computation.4 | custom fusion | flops 393216 | bytes 2228736 | tf_op jit(solution)/shard_map/scatter-add | solution.py:56
  74.6 1.9 %collective-permute-start.12 = (f32[16,16,128]{2,1,0:T(8,128)S(1)}, f32[16,16,128]{2,1,0:T(8,128)S(1)}, u32[]{:S(2)}, u32[]{:S(2)}) collective-permute-start(f32[16,16,128]{2,1,0:T(8,128)S(1)} %bitcast.139), channel_id=1, source_target_pairs={{1,0},{2,1},{3,2},{4,3},{5,4},{6,5},{7,6},{8,7},{9,8},{10,9},{11,1... | collective-permute-start | bytes 393224 | tf_op jit(solution)/shard_map/ppermute | solution.py:12
  77.3 7.5 %collective-permute-start.13 = (f32[16,16,128]{2,1,0:T(8,128)S(1)}, f32[16,16,128]{2,1,0:T(8,128)S(1)}, u32[]{:S(2)}, u32[]{:S(2)}) collective-permute-start(f32[16,16,128]{2,1,0:T(8,128)S(1)} %bitcast.142), channel_id=1, source_target_pairs={{2,0},{3,1},{4,2},{5,3},{6,4},{7,5},{8,6},{9,7},{10,8},{11,9},{12,... | collective-permute-start | bytes 393224 | tf_op jit(solution)/shard_map/ppermute | solution.py:12
  84.9 2.3 %collective-permute-start.14 = (f32[16,16,128]{2,1,0:T(8,128)S(1)}, f32[16,16,128]{2,1,0:T(8,128)S(1)}, u32[]{:S(2)}, u32[]{:S(2)}) collective-permute-start(f32[16,16,128]{2,1,0:T(8,128)S(1)} %bitcast.141), channel_id=1, source_target_pairs={{3,0},{4,1},{5,2},{6,3},{7,4},{8,5},{9,6},{10,7},{11,8},{12,9},{13... | collective-permute-start | bytes 393224 | tf_op jit(solution)/shard_map/ppermute | solution.py:12
  87.2 5.4 %collective-permute-start.15 = (f32[16,16,128]{2,1,0:T(8,128)S(1)}, f32[16,16,128]{2,1,0:T(8,128)S(1)}, u32[]{:S(2)}, u32[]{:S(2)}) collective-permute-start(f32[16,16,128]{2,1,0:T(8,128)S(1)} %bitcast.140), channel_id=1, source_target_pairs={{4,0},{5,1},{6,2},{7,3},{8,4},{9,5},{10,6},{11,7},{12,8},{13,9},{1... | collective-permute-start | bytes 393224 | tf_op jit(solution)/shard_map/ppermute | solution.py:12
  92.7 0.8 gather_fusion.1
  93.8 6.2 %multiply_reduce_fusion = f32[16,16,128]{2,1,0:T(8,128)S(1)} fusion(bf16[16,12,16,128]{3,2,1,0:T(8,128)(2,1)S(1)} %bitcast.137, bf16[16,12,128,128]{3,2,1,0:T(8,128)(2,1)} %param.7, f32[16,12]{1,0:T(8,128)S(1)} %compare_select_fusion), kind=kOutput, calls=%fused_computation.10 | convolution fusion | flops 101416960 | bytes 7209728 | tf_op jit(solution)/shard_map/rkvc,rkac->rkva/dot_general | solution.py:48
  100.0 0.7 copy_bitcast_fusion
  (54 shorter events, 3.3 us)
Async XLA Ops:
  0.6 0.8 copy-start
  1.5 32.0 %collective-permute-start = (bf16[16,16,128]{2,1,0:T(8,128)(2,1)S(1)}, bf16[16,16,128]{2,1,0:T(8,128)(2,1)S(1)}, u32[]{:S(2)}, u32[]{:S(2)}) collective-permute-start(bf16[16,16,128]{2,1,0:T(8,128)(2,1)S(1)} %bitcast_bitcast_fusion.1), channel_id=1, source_target_pairs={{0,4},{1,5},{2,6},{3,7},{4,8},{5,9},{6,10},{7,11},{8,12},{9,13},{1... | collective-permute-start | bytes 196616 | tf_op jit(solution)/shard_map/ppermute | solution.py:12
  6.4 34.0 %collective-permute-start.1 = (bf16[16,16,128]{2,1,0:T(8,128)(2,1)S(1)}, bf16[16,16,128]{2,1,0:T(8,128)(2,1)S(1)}, u32[]{:S(2)}, u32[]{:S(2)}) collective-permute-start(bf16[16,16,128]{2,1,0:T(8,128)(2,1)S(1)} %bitcast_bitcast_fusion.1), channel_id=1, source_target_pairs={{0,3},{1,4},{2,5},{3,6},{4,7},{5,8},{6,9},{7,10},{8,11},{9,12},{10... | collective-permute-start | bytes 196616 | tf_op jit(solution)/shard_map/ppermute | solution.py:12
  13.4 29.0 %collective-permute-start.2 = (bf16[16,16,128]{2,1,0:T(8,128)(2,1)S(1)}, bf16[16,16,128]{2,1,0:T(8,128)(2,1)S(1)}, u32[]{:S(2)}, u32[]{:S(2)}) collective-permute-start(bf16[16,16,128]{2,1,0:T(8,128)(2,1)S(1)} %bitcast_bitcast_fusion.1), channel_id=1, source_target_pairs={{0,2},{1,3},{2,4},{3,5},{4,6},{5,7},{6,8},{7,9},{8,10},{9,11},{10,... | collective-permute-start | bytes 196616 | tf_op jit(solution)/shard_map/ppermute | solution.py:12
  16.0 30.2 %collective-permute-start.3 = (bf16[16,16,128]{2,1,0:T(8,128)(2,1)S(1)}, bf16[16,16,128]{2,1,0:T(8,128)(2,1)S(1)}, u32[]{:S(2)}, u32[]{:S(2)}) collective-permute-start(bf16[16,16,128]{2,1,0:T(8,128)(2,1)S(1)} %bitcast_bitcast_fusion.1), channel_id=1, source_target_pairs={{0,1},{1,2},{2,3},{3,4},{4,5},{5,6},{6,7},{7,8},{8,9},{9,10},{10,1... | collective-permute-start | bytes 196616 | tf_op jit(solution)/shard_map/ppermute | solution.py:12
  19.5 3.7 %copy-start.1 = (s32[192,1]{0,1:T(1,128)}, s32[192,1]{0,1:T(1,128)S(1)}, u32[]{:S(2)}) copy-start(s32[192,1]{0,1:T(1,128)S(1)} %compare_select_fusion.1) | copy-start | bytes 2308
  27.6 26.1 %collective-permute-start.4 = (f32[16,16,128]{2,1,0:T(8,128)}, f32[16,16,128]{2,1,0:T(8,128)S(1)}, u32[]{:S(2)}, u32[]{:S(2)}) collective-permute-start(f32[16,16,128]{2,1,0:T(8,128)} %bitcast.29), channel_id=1, source_target_pairs={{1,0},{2,1},{3,2},{4,3},{5,4},{6,5},{7,6},{8,7},{9,8},{10,9},{11,1... | collective-permute-start | bytes 393224 | tf_op jit(solution)/shard_map/ppermute | solution.py:12
  33.5 20.2 %collective-permute-start.5 = (f32[16,16,128]{2,1,0:T(8,128)}, f32[16,16,128]{2,1,0:T(8,128)}, u32[]{:S(2)}, u32[]{:S(2)}) collective-permute-start(f32[16,16,128]{2,1,0:T(8,128)} %bitcast.31), channel_id=1, source_target_pairs={{2,0},{3,1},{4,2},{5,3},{6,4},{7,5},{8,6},{9,7},{10,8},{11,9},{12,... | collective-permute-start | bytes 393224 | tf_op jit(solution)/shard_map/ppermute | solution.py:12
  40.4 13.3 %collective-permute-start.6 = (f32[16,16,128]{2,1,0:T(8,128)}, f32[16,16,128]{2,1,0:T(8,128)}, u32[]{:S(2)}, u32[]{:S(2)}) collective-permute-start(f32[16,16,128]{2,1,0:T(8,128)} %bitcast.33), channel_id=1, source_target_pairs={{3,0},{4,1},{5,2},{6,3},{7,4},{8,5},{9,6},{10,7},{11,8},{12,9},{13... | collective-permute-start | bytes 393224 | tf_op jit(solution)/shard_map/ppermute | solution.py:12
  42.3 12.3 %collective-permute-start.7 = (f32[16,16,128]{2,1,0:T(8,128)}, f32[16,16,128]{2,1,0:T(8,128)}, u32[]{:S(2)}, u32[]{:S(2)}) collective-permute-start(f32[16,16,128]{2,1,0:T(8,128)} %bitcast.35), channel_id=1, source_target_pairs={{4,0},{5,1},{6,2},{7,3},{8,4},{9,5},{10,6},{11,7},{12,8},{13,9},{1... | collective-permute-start | bytes 393224 | tf_op jit(solution)/shard_map/ppermute | solution.py:12
  46.2 21.7 %slice-start = ((s8[6291456]{0:T(1024)(128)(4,1)}), s8[2097152]{0:T(1024)(128)(4,1)S(1)}, s32[]{:S(2)}) async-start(s8[6291456]{0:T(1024)(128)(4,1)} %bitcast.133), calls=%async_computation | async-start | bytes 4194304
  47.3 20.6 %slice-start.1 = ((s8[6291456]{0:T(1024)(128)(4,1)}), s8[4194304]{0:T(1024)(128)(4,1)S(1)}, s32[]{:S(2)}) async-start(s8[6291456]{0:T(1024)(128)(4,1)} %bitcast.133), calls=%async_computation.1 | async-start | bytes 8388608
  55.7 21.6 %collective-permute-start.8 = (bf16[16,16,128]{2,1,0:T(8,128)(2,1)S(1)}, bf16[16,16,128]{2,1,0:T(8,128)(2,1)S(1)}, u32[]{:S(2)}, u32[]{:S(2)}) collective-permute-start(bf16[16,16,128]{2,1,0:T(8,128)(2,1)S(1)} %get-tuple-element.3), channel_id=1, source_target_pairs={{0,4},{1,5},{2,6},{3,7},{4,8},{5,9},{6,10},{7,11},{8,12},{9,13},{1... | collective-permute-start | bytes 196616 | tf_op jit(solution)/shard_map/ppermute | solution.py:12
  58.2 26.7 %collective-permute-start.9 = (bf16[16,16,128]{2,1,0:T(8,128)(2,1)S(1)}, bf16[16,16,128]{2,1,0:T(8,128)(2,1)S(1)}, u32[]{:S(2)}, u32[]{:S(2)}) collective-permute-start(bf16[16,16,128]{2,1,0:T(8,128)(2,1)S(1)} %get-tuple-element.3), channel_id=1, source_target_pairs={{0,3},{1,4},{2,5},{3,6},{4,7},{5,8},{6,9},{7,10},{8,11},{9,12},{10... | collective-permute-start | bytes 196616 | tf_op jit(solution)/shard_map/ppermute | solution.py:12
  63.5 23.7 %collective-permute-start.10 = (bf16[16,16,128]{2,1,0:T(8,128)(2,1)S(1)}, bf16[16,16,128]{2,1,0:T(8,128)(2,1)S(1)}, u32[]{:S(2)}, u32[]{:S(2)}) collective-permute-start(bf16[16,16,128]{2,1,0:T(8,128)(2,1)S(1)} %get-tuple-element.3), channel_id=1, source_target_pairs={{0,2},{1,3},{2,4},{3,5},{4,6},{5,7},{6,8},{7,9},{8,10},{9,11},{10,... | collective-permute-start | bytes 196616 | tf_op jit(solution)/shard_map/ppermute | solution.py:12
  65.4 27.2 %collective-permute-start.11 = (bf16[16,16,128]{2,1,0:T(8,128)(2,1)S(1)}, bf16[16,16,128]{2,1,0:T(8,128)(2,1)S(1)}, u32[]{:S(2)}, u32[]{:S(2)}) collective-permute-start(bf16[16,16,128]{2,1,0:T(8,128)(2,1)S(1)} %get-tuple-element.3), channel_id=1, source_target_pairs={{0,1},{1,2},{2,3},{3,4},{4,5},{5,6},{6,7},{7,8},{8,9},{9,10},{10,1... | collective-permute-start | bytes 196616 | tf_op jit(solution)/shard_map/ppermute | solution.py:12
  74.6 25.4 %collective-permute-start.12 = (f32[16,16,128]{2,1,0:T(8,128)S(1)}, f32[16,16,128]{2,1,0:T(8,128)S(1)}, u32[]{:S(2)}, u32[]{:S(2)}) collective-permute-start(f32[16,16,128]{2,1,0:T(8,128)S(1)} %bitcast.139), channel_id=1, source_target_pairs={{1,0},{2,1},{3,2},{4,3},{5,4},{6,5},{7,6},{8,7},{9,8},{10,9},{11,1... | collective-permute-start | bytes 393224 | tf_op jit(solution)/shard_map/ppermute | solution.py:12
  77.3 22.6 %collective-permute-start.13 = (f32[16,16,128]{2,1,0:T(8,128)S(1)}, f32[16,16,128]{2,1,0:T(8,128)S(1)}, u32[]{:S(2)}, u32[]{:S(2)}) collective-permute-start(f32[16,16,128]{2,1,0:T(8,128)S(1)} %bitcast.142), channel_id=1, source_target_pairs={{2,0},{3,1},{4,2},{5,3},{6,4},{7,5},{8,6},{9,7},{10,8},{11,9},{12,... | collective-permute-start | bytes 393224 | tf_op jit(solution)/shard_map/ppermute | solution.py:12
  84.9 15.1 %collective-permute-start.14 = (f32[16,16,128]{2,1,0:T(8,128)S(1)}, f32[16,16,128]{2,1,0:T(8,128)S(1)}, u32[]{:S(2)}, u32[]{:S(2)}) collective-permute-start(f32[16,16,128]{2,1,0:T(8,128)S(1)} %bitcast.141), channel_id=1, source_target_pairs={{3,0},{4,1},{5,2},{6,3},{7,4},{8,5},{9,6},{10,7},{11,8},{12,9},{13... | collective-permute-start | bytes 393224 | tf_op jit(solution)/shard_map/ppermute | solution.py:12
  87.2 12.7 %collective-permute-start.15 = (f32[16,16,128]{2,1,0:T(8,128)S(1)}, f32[16,16,128]{2,1,0:T(8,128)S(1)}, u32[]{:S(2)}, u32[]{:S(2)}) collective-permute-start(f32[16,16,128]{2,1,0:T(8,128)S(1)} %bitcast.140), channel_id=1, source_target_pairs={{4,0},{5,1},{6,2},{7,3},{8,4},{9,5},{10,6},{11,7},{12,8},{13,9},{1... | collective-permute-start | bytes 393224 | tf_op jit(solution)/shard_map/ppermute | solution.py:12
where the time goes:
time: 101 us
  starting transfers between devices  60.7 us (60%)
  matrix products  18.3 us (18%)
  other arithmetic  11.9 us (12%)
  local copies, waits for them, and re-layouts  6.36 us (6%)
  between operations  2.41 us (2%)
  waiting for transfers between devices  1.02 us (1%)
    ppermute x16, starting transfers between devices, passed_along(): return lax.ppermute(block, axis, route)  60.7 us
    dot_general x2, matrix products, apply_local(): jnp.einsum('rkvc,rkac->rkva', picked, matrix_tiles, preferred_element_typ...  12.5 us
    scatter-add x2, other arithmetic, apply_local(): jnp.zeros((slot_count, count_vec * width), jnp.float32).at[flat_slots]  8.05 us
    dot_general x2, matrix products, apply_local(): jnp.einsum('rva,rkac->rkvc', blocks, matrix_tiles, preferred_element_type...  5.81 us
    unnamed x28, local copies, waits for them, and re-layouts  3.92 us
  transfers between devices with their start and end apart: 16, of which 1 were waited for; matrix products, arithmetic and copies ran while one was open for 34% of the time, Pallas kernels for 0%

commit v1 on v0

v1 whole, which is shorter than its diff:
```python
import functools

import jax
import jax.numpy as jnp
from jax import lax
from jax.experimental import pallas as pl
from jax.experimental.pallas import tpu as pltpu
from jax.sharding import PartitionSpec as P

SPAN = 4
CHAINS = 2
TOP = 32766.0
MESH = pl.DeviceIdType.MESH
F32 = jnp.float32
LAST_ROW = 16
SLOT_ROW = LAST_ROW + 8 * CHAINS
ON_LAST = (((1,), (1,)), ((), ()))


def kernel(
    n,
    tiles_hbm,
    cols_v,
    cols_s,
    vec_v,
    center_s,
    half_s,
    out1,
    out2,
    tiles,
    win0,
    win1,
    sums,
    ahead,
    total,
    coded,
    landed,
    tab_v,
    tab_s,
    tile_sem,
    tab_sem,
    xsend,
    xrecv,
    psend,
    precv,
):
    rows, kt, width, _ = tiles.shape
    nv = vec_v.shape[0]
    half = rows // CHAINS
    none = half * kt
    me = lax.axis_index("tri")
    lowest = (me - SPAN) * rows

    def load(r):
        return pltpu.make_async_copy(tiles_hbm.at[r], tiles.at[r], tile_sem.at[r])

    for j in range(half):
        for c in range(CHAINS):
            load(c * half + j).start()

    barrier = pltpu.get_barrier_semaphore()
    for o in range(1, SPAN + 1):
        for d in (o, n - o):
            pl.semaphore_signal(
                barrier, inc=1, device_id=(lax.rem(me + d, n),), device_id_type=MESH
            )

    own = SPAN * rows
    win = (win0, win1)
    for r in range(rows):
        win0[own + r] = vec_v[:, r * width : (r + 1) * width]

    sums[:, none] = jnp.zeros((CHAINS, nv, width), F32)
    tid = lax.broadcasted_iota(jnp.int32, (half, kt), 0) * kt + lax.broadcasted_iota(
        jnp.int32, (half, kt), 1
    )
    lane = lax.broadcasted_iota(jnp.int32, (8, 128), 1)
    slots = jnp.clip(cols_v[...] - lowest, 0, (SPAN + 1) * rows - 1)
    tab_v[SLOT_ROW : SLOT_ROW + rows, 0:kt] = slots
    for c in range(CHAINS):
        mine = slots[c * half : (c + 1) * half]

        def note(j, carry):
            prev, last = carry
            for k in range(kt):
                s = cols_s[c * half + j, k] - lowest
                t = j * kt + k
                prev = jnp.where((mine == s) & (tid > t), t, prev)
                last = jnp.where(lane == s, t, last)
            return prev, last

        prev, last = lax.fori_loop(
            0,
            half,
            note,
            (jnp.full((half, kt), none, jnp.int32), jnp.full((8, 128), none, jnp.int32)),
        )
        tab_v[c * half : (c + 1) * half, 0:kt] = prev
        tab_v[LAST_ROW + 8 * c : LAST_ROW + 8 * (c + 1), :] = last
    tab_copy = pltpu.make_async_copy(tab_v, tab_s, tab_sem)
    tab_copy.start()

    pl.semaphore_wait(barrier, 2 * SPAN)

    def vector_copy(step, o):
        return pltpu.make_async_remote_copy(
            src_ref=win[step].at[pl.ds(own, rows)],
            dst_ref=win[step].at[pl.ds((SPAN - o) * rows, rows)],
            send_sem=xsend.at[step, o - 1],
            recv_sem=xrecv.at[step, o - 1],
            device_id=(lax.rem(me + o, n),),
            device_id_type=MESH,
        )

    def product_copy(step, g):
        return pltpu.make_async_remote_copy(
            src_ref=coded.at[step, g],
            dst_ref=landed.at[step, g],
            send_sem=psend.at[step, g],
            recv_sem=precv.at[step, g],
            device_id=(lax.rem(me + n - SPAN + g, n),),
            device_id_type=MESH,
        )

    def transposed_products(step):
        def body(j, carry):
            for c in range(CHAINS):
                r = c * half + j
                if step == 0:
                    load(r).wait()
                x = win[step][own + r]
                for k in range(0, kt, 2):
                    pair = jnp.concatenate([tiles[r, k], tiles[r, k + 1]], axis=1)
                    both = jnp.dot(x, pair, preferred_element_type=F32)
                    for i in range(2):
                        s = tab_s[SLOT_ROW + r, k + i]
                        weight = jnp.where(s == own + r, 0.5, 1.0).astype(F32)
                        part = both[:, i * width : (i + 1) * width] * weight
                        before = tab_s[r, k + i]
                        sums[c, j * kt + k + i] = part + sums[c, before]
            return carry

        lax.fori_loop(0, half, body, 0)

    def slot_sum(s):
        return sum(sums[c, tab_s[LAST_ROW + 8 * c, s]] for c in range(CHAINS))

    def send_products(step):
        def body(g, carry):
            most = jnp.zeros((nv, width), F32)
            for r in range(rows):
                v = slot_sum(g * rows + r)
                total[r] = v
                most = jnp.maximum(most, jnp.abs(v))
            peak = jnp.maximum(jnp.max(most, axis=1, keepdims=True), 1e-30)
            power = jnp.broadcast_to(jnp.ceil(jnp.log2(peak)), (nv, width))
            scale = jnp.exp2(-power) * TOP
            for r in range(rows):
                coded[step, g, r] = (
                    jnp.round(total[r] * scale).astype(jnp.int32).astype(jnp.int16)
                )
            coded[step, g, rows] = power.astype(jnp.int32).astype(jnp.int16)
            product_copy(step, g).start()
            return carry

        lax.fori_loop(0, SPAN, body, 0)

    def forward(step):
        def body(r, carry):
            picked = []
            for k in range(kt):
                s = tab_s[SLOT_ROW + r, k]
                weight = jnp.where(s == own + r, 0.5, 1.0).astype(F32)
                picked.append(win[step][s] * jnp.full((nv, width), weight).astype(jnp.bfloat16))
            x = jnp.concatenate(picked, axis=1)
            w = jnp.concatenate([tiles[r, k] for k in range(kt)], axis=1)
            ahead[r] = lax.dot_general(x, w, ON_LAST, preferred_element_type=F32)
            return carry

        lax.fori_loop(0, rows, body, 0)

    center = center_s[0]
    inv = 1.0 / jnp.full((nv, width), half_s[0], F32)

    for step in range(2):
        for o in range(1, SPAN + 1):
            vector_copy(step, o).start()
        if step == 0:
            tab_copy.wait()
        transposed_products(step)
        send_products(step)
        for o in range(1, SPAN + 1):
            vector_copy(step, o).wait_recv()
        forward(step)
        scales = []
        for g in range(SPAN):
            product_copy(step, g).wait_recv()
        for g in range(SPAN):
            power = landed[step, g, rows].astype(jnp.int32).astype(F32)
            scales.append(jnp.exp2(power) * (1.0 / TOP))
        for r in range(rows):
            cut = slice(r * width, (r + 1) * width)
            v = ahead[r] + slot_sum(own + r)
            for g in range(SPAN):
                v = v + landed[step, g, r].astype(jnp.int32).astype(F32) * scales[g]
            x0 = win0[own + r].astype(F32)
            if step == 0:
                first = (v - center * x0) * inv
                out1[:, cut] = first
                win1[own + r] = first.astype(jnp.bfloat16)
            else:
                out2[:, cut] = 2.0 * (v - center * out1[:, cut]) * inv - x0

    for step in range(2):
        for o in range(1, SPAN + 1):
            vector_copy(step, o).wait_send()
        for g in range(SPAN):
            product_copy(step, g).wait_send()


def per_device(n, matrix_tiles, columns, vectors, center, halfwidth):
    rows, kt, width, _ = matrix_tiles.shape
    nv = vectors.shape[0]
    vmem = pl.BlockSpec(memory_space=pltpu.VMEM)
    smem = pl.BlockSpec(memory_space=pltpu.SMEM)
    out = jax.ShapeDtypeStruct(vectors.shape, F32)
    chain = rows // CHAINS * kt
    return pl.pallas_call(
        functools.partial(kernel, n),
        out_shape=(out, out),
        in_specs=[pl.BlockSpec(memory_space=pl.ANY), vmem, smem, vmem, smem, smem],
        out_specs=(vmem, vmem),
        scratch_shapes=[
            pltpu.VMEM(matrix_tiles.shape, jnp.bfloat16),
            pltpu.VMEM(((SPAN + 1) * rows, nv, width), jnp.bfloat16),
            pltpu.VMEM(((SPAN + 1) * rows, nv, width), jnp.bfloat16),
            pltpu.VMEM((CHAINS, chain + 1, nv, width), F32),
            pltpu.VMEM((rows, nv, width), F32),
            pltpu.VMEM((rows, nv, width), F32),
            pltpu.VMEM((2, SPAN, rows + 1, nv, width), jnp.int16),
            pltpu.VMEM((2, SPAN, rows + 1, nv, width), jnp.int16),
            pltpu.VMEM((SLOT_ROW + rows, 128), jnp.int32),
            pltpu.SMEM((SLOT_ROW + rows, 128), jnp.int32),
            pltpu.SemaphoreType.DMA((rows,)),
            pltpu.SemaphoreType.DMA,
            pltpu.SemaphoreType.DMA((2, SPAN)),
            pltpu.SemaphoreType.DMA((2, SPAN)),
            pltpu.SemaphoreType.DMA((2, SPAN)),
            pltpu.SemaphoreType.DMA((2, SPAN)),
        ],
        compiler_params=pltpu.CompilerParams(
            collective_id=0, has_side_effects=True, vmem_limit_bytes=32 << 20
        ),
    )(matrix_tiles, columns, columns, vectors, center, halfwidth)


def solution(mesh):
    placed = (P("tri", None, None, None), P("tri", None), P(None, "tri"), P(), P())
    return jax.shard_map(
        functools.partial(per_device, mesh.shape["tri"]),
        mesh=mesh,
        in_specs=placed,
        out_specs=(P(None, "tri"), P(None, "tri")),
        check_vma=False,
    )
```

time: 101 us -> 52.3 us (0.52)
  the two profiles are of different devices: /device:TPU:25 before, /device:TPU:33 now
where the time goes in v1:
time: 52.3 us; the launch traced here: 52.1 us
  Pallas kernels  44.6 us (85%)
  local copies, waits for them, and re-layouts  5.63 us (11%)
  between operations  1.94 us (4%)
    pallas_call x1, Pallas kernels, per_device(): pl.pallas_call(functools.partial(kernel, n), out_shape=(out, out), in_spe...  44.6 us
    unnamed x8, local copies, waits for them, and re-layouts  5.63 us

profile of v1, /device:TPU:33, one launch (start us, length us, event | category | flops | bytes accessed | tf_op | source)
XLA Modules:
  0.0 52.1 jit_solution(5148174479270510329)
XLA Ops:
  1.9 0.0 copy-start
  1.9 2.8 %copy-done = bf16[16,12,128,128]{3,2,1,0:T(8,128)(2,1)S(1)} copy-done((bf16[16,12,128,128]{3,2,1,0:T(8,128)(2,1)S(1)}, bf16[16,12,128,128]{3,2,1,0:T(8,128)(2,1)}, u32[]{:S(2)}) %copy-start) | copy-done | bytes 6291480
  4.7 0.0 copy-start.1
  4.7 0.8 %copy-done.1 = bf16[16,2048]{1,0:T(8,128)(2,1)S(1)} copy-done((bf16[16,2048]{1,0:T(8,128)(2,1)S(1)}, bf16[16,2048]{1,0:T(8,128)(2,1)}, u32[]{:S(2)}) %copy-start.1) | copy-done | bytes 65560
  5.5 0.0 copy-start.2
  5.5 0.7 %copy-done.2 = s32[16,12]{1,0:T(8,128)S(1)} copy-done((s32[16,12]{1,0:T(8,128)S(1)}, s32[16,12]{1,0:T(8,128)}, u32[]{:S(2)}) %copy-start.2) | copy-done | bytes 792
  6.2 44.6 %shard_map.68 = (f32[16,2048]{1,0:T(8,128)S(1)}, f32[16,2048]{1,0:T(8,128)S(1)}) custom-call(bf16[16,12,128,128]{3,2,1,0:T(8,128)(2,1)S(1)} %copy-done, s32[16,12]{1,0:T(8,128)S(1)} %copy-done.2, s32[16,12]{1,0:T(8,128)S(1)} %copy-done.2, bf16[16,2048]{1,0:T(8,128)(2,1)S(1)} %copy-done.1, f32[1]{0:T(128)S(6)} %copy.9.center_s, f32[1]{0:T(128)S(6)} %copy.10.half_s), custom_call_target="tpu_custom_call" | custom-call | tf_op jit(solution)/shard_map/pallas_call | solution.py:228
  50.8 0.7 %copy.11 = f32[16,2048]{1,0:T(8,128)} copy(f32[16,2048]{1,0:T(8,128)S(1)} %get-tuple-element.4) | data formatting | bytes 262144
  51.5 0.7 %copy.12 = f32[16,2048]{1,0:T(8,128)} copy(f32[16,2048]{1,0:T(8,128)S(1)} %get-tuple-element.5) | data formatting | bytes 262144
Async XLA Ops:
  1.9 2.8 %copy-start = (bf16[16,12,128,128]{3,2,1,0:T(8,128)(2,1)S(1)}, bf16[16,12,128,128]{3,2,1,0:T(8,128)(2,1)}, u32[]{:S(2)}) copy-start(bf16[16,12,128,128]{3,2,1,0:T(8,128)(2,1)} %tiles_hbm.1) | copy-start | bytes 18874372
  4.7 0.8 %copy-start.1 = (bf16[16,2048]{1,0:T(8,128)(2,1)S(1)}, bf16[16,2048]{1,0:T(8,128)(2,1)}, u32[]{:S(2)}) copy-start(bf16[16,2048]{1,0:T(8,128)(2,1)} %vec_v.1) | copy-start | bytes 196612
  5.5 0.7 %copy-start.2 = (s32[16,12]{1,0:T(8,128)S(1)}, s32[16,12]{1,0:T(8,128)}, u32[]{:S(2)}) copy-start(s32[16,12]{1,0:T(8,128)} %cols_s.1) | copy-start | bytes 2308

commit v2 on v1

v2 whole, which is shorter than its diff:
```python
import functools

import jax
import jax.numpy as jnp
from jax import lax
from jax.experimental import pallas as pl
from jax.experimental.pallas import tpu as pltpu
from jax.sharding import PartitionSpec as P

SPAN = 4
BEHIND_PARTS = 2
FORWARD_PARTS = 2
CHAINS = 2
TOP = 32766.0
MESH = pl.DeviceIdType.MESH
F32 = jnp.float32
LAST_ROW = 16
SLOT_ROW = LAST_ROW + 8 * CHAINS
ON_LAST = (((1,), (1,)), ((), ()))


def kernel(
    n,
    tiles_hbm,
    cols_hbm,
    vec_hbm,
    center_hbm,
    half_hbm,
    out1,
    out2,
    cols_v,
    cols_s,
    vec_v,
    center_s,
    half_s,
    tiles,
    win0,
    win1,
    sums,
    ahead,
    total,
    staged,
    shared,
    coded,
    landed,
    tab_v,
    tab_s,
    tile_sem,
    small_sem,
    tab_sem,
    xsend,
    xrecv,
    ssend,
    srecv,
    psend,
    precv,
):
    rows, kt, width, _ = tiles.shape
    nv = vec_v.shape[0]
    half = rows // CHAINS
    none = half * kt
    me = lax.axis_index("tri")
    core = lax.rem(me, 2)
    other = me + 1 - 2 * core
    lowest = (me - SPAN) * rows

    def exists(d):
        return (me + d >= 0) & (me + d < n)


    def load(r):
        return pltpu.make_async_copy(tiles_hbm.at[r], tiles.at[r], tile_sem.at[r])

    def small(i, src, dst):
        return pltpu.make_async_copy(src, dst, small_sem.at[i])

    smalls = [
        small(0, cols_hbm, cols_s),
        small(1, cols_hbm, cols_v),
        small(2, vec_hbm, vec_v),
        small(3, center_hbm, center_s),
        small(4, half_hbm, half_s),
    ]
    for copy in smalls:
        copy.start()
    for j in range(half):
        for c in range(CHAINS):
            load(c * half + j).start()

    barrier = pltpu.get_barrier_semaphore()
    pl.semaphore_signal(barrier, inc=1, device_id=(other,), device_id_type=MESH)
    for d in (2, -2, 4, -4):

        @pl.when(exists(d))
        def _():
            pl.semaphore_signal(barrier, inc=1, device_id=(me + d,), device_id_type=MESH)

    own = SPAN * rows
    win = (win0, win1)
    smalls[2].wait()
    for r in range(rows):
        win0[own + r] = vec_v[:, r * width : (r + 1) * width]
    for i, d in enumerate((4, 2)):

        @pl.when(jnp.logical_not(exists(d)))
        def _():
            for step in range(2):
                landed[step, i] = jnp.zeros(landed.shape[2:], landed.dtype)

    for step in range(2):
        shared[step, 2 * core] = jnp.zeros(shared.shape[2:], F32)

    greeted = 1 + jnp.minimum(me // 2, 2) + jnp.minimum((n - 1 - me) // 2, 2)
    pl.semaphore_wait(barrier, greeted)

    def vector_copy(step, i, src, dst, to):
        return pltpu.make_async_remote_copy(
            src_ref=win[step].at[pl.ds(src * rows, rows)],
            dst_ref=win[step].at[pl.ds(dst * rows, rows)],
            send_sem=xsend.at[step, i],
            recv_sem=xrecv.at[step, dst],
            device_id=(to,),
            device_id_type=MESH,
        )

    def vector_sends(step):
        return [
            (core == 0, vector_copy(step, 0, SPAN, SPAN - 1, other)),
            (exists(4), vector_copy(step, 1, SPAN, SPAN - 4, me + 4)),
            (exists(2), vector_copy(step, 2, SPAN, SPAN - 2, me + 2)),
        ]

    def vector_hands(step):
        return [
            (2, vector_copy(step, 3, 2, 1 + 2 * core, other), exists(-2)),
            (0, vector_copy(step, 4, 0, 1, other), exists(-4) & (core == 1)),
        ]

    def await_vectors(step, g):
        @pl.when(exists(g - SPAN))
        def _():
            vector_copy(step, 0, SPAN, g, other).wait_recv()

    def send_vectors(step):
        for wanted, copy in vector_sends(step):
            pl.when(wanted)(copy.start)

    send_vectors(0)

    for c in range(CHAINS):
        sums[c][none] = jnp.zeros((nv, width), F32)
    for copy in smalls[:2]:
        copy.wait()
    tid = lax.broadcasted_iota(jnp.int32, (half, kt), 0) * kt + lax.broadcasted_iota(
        jnp.int32, (half, kt), 1
    )
    lane = lax.broadcasted_iota(jnp.int32, (8, 128), 1)
    slots = jnp.clip(cols_v[...] - lowest, 0, (SPAN + 1) * rows - 1)
    tab_v[SLOT_ROW : SLOT_ROW + rows, 0:kt] = slots
    for c in range(CHAINS):
        mine = slots[c * half : (c + 1) * half]

        def note(j, carry):
            prev, last = carry
            for k in range(kt):
                s = cols_s[c * half + j, k] - lowest
                t = j * kt + k
                prev = jnp.where((mine == s) & (tid > t), t, prev)
                last = jnp.where(lane == s, t, last)
            return prev, last

        prev, last = lax.fori_loop(
            0,
            half,
            note,
            (jnp.full((half, kt), none, jnp.int32), jnp.full((8, 128), none, jnp.int32)),
        )
        tab_v[c * half : (c + 1) * half, 0:kt] = prev
        tab_v[LAST_ROW + 8 * c : LAST_ROW + 8 * (c + 1), :] = last
    tab_copy = pltpu.make_async_copy(tab_v, tab_s, tab_sem)
    tab_copy.start()

    def share_copy(step, i):
        return pltpu.make_async_remote_copy(
            src_ref=staged.at[step, i],
            dst_ref=shared.at[step, core + i],
            send_sem=ssend.at[step, i],
            recv_sem=srecv.at[step, core + i],
            device_id=(other,),
            device_id_type=MESH,
        )

    def await_share(step, i):
        pltpu.make_async_remote_copy(
            src_ref=staged.at[step, 0],
            dst_ref=shared.at[step, i],
            send_sem=ssend.at[step, 0],
            recv_sem=srecv.at[step, i],
            device_id=(other,),
            device_id_type=MESH,
        ).wait_recv()

    def product_copy(step, i):
        return pltpu.make_async_remote_copy(
            src_ref=coded.at[step, i],
            dst_ref=landed.at[step, i],
            send_sem=psend.at[step, i],
            recv_sem=precv.at[step, i],
            device_id=(me - SPAN + 2 * i,),
            device_id_type=MESH,
        )

    def transposed_products(step):
        def body(part, carry):
            for i in range(half // BEHIND_PARTS):
                j = part * (half // BEHIND_PARTS) + i
                if step == 0:
                    for c in range(CHAINS):
                        load(c * half + j).wait()
                for k in range(0, kt, 2):
                    for c in range(CHAINS):
                        add_pair(step, c, j, k)
            return carry

        lax.fori_loop(0, BEHIND_PARTS, body, 0)

    def add_pair(step, c, j, k):
        r = c * half + j
        pair = jnp.concatenate([tiles[r, k], tiles[r, k + 1]], axis=1)
        both = jnp.dot(win[step][own + r], pair, preferred_element_type=F32)
        for i in range(2):
            slot = tab_s[SLOT_ROW + r, k + i]
            weight = jnp.where(slot == own + r, 0.5, 1.0).astype(F32)
            part = both[:, i * width : (i + 1) * width] * weight
            before = tab_s[r, k + i]
            sums[c][j * kt + k + i] = part + sums[c][before]

    def slot_sum(s):
        return sum(sums[c][tab_s[LAST_ROW + 8 * c, s]] for c in range(CHAINS))

    def send_products(step):
        for i in range(2):
            for r in range(rows):
                staged[step, i, r] = slot_sum((2 * i + 1) * rows + r)
            share_copy(step, i).start()
        for i in range(2):
            if i == 0:
                pl.when(core == 1)(lambda: await_share(step, 0))
            else:
                await_share(step, 1)
            most = jnp.zeros((nv, width), F32)
            for r in range(rows):
                v = slot_sum(2 * i * rows + r) + shared[step, i, r]
                total[r] = v
                most = jnp.maximum(most, jnp.abs(v))
            peak = jnp.maximum(jnp.max(most, axis=1, keepdims=True), 1e-30)
            power = jnp.broadcast_to(jnp.ceil(jnp.log2(peak)), (nv, width))
            scale = jnp.exp2(-power) * TOP
            for r in range(rows):
                coded[step, i, r] = (
                    jnp.round(total[r] * scale).astype(jnp.int32).astype(jnp.int16)
                )
            coded[step, i, rows] = power.astype(jnp.int32).astype(jnp.int16)
            pl.when(exists(2 * i - SPAN))(product_copy(step, i).start)

    def forward(step):
        def body(part, carry):
            for i in range(rows // FORWARD_PARTS):
                r = part * (rows // FORWARD_PARTS) + i
                picked = []
                for k in range(kt):
                    s = tab_s[SLOT_ROW + r, k]
                    weight = jnp.full((nv, width), jnp.where(s == own + r, 0.5, 1.0), F32)
                    picked.append(win[step][s] * weight.astype(jnp.bfloat16))
                x = jnp.concatenate(picked, axis=1)
                w = jnp.concatenate([tiles[r, k] for k in range(kt)], axis=1)
                ahead[r] = lax.dot_general(x, w, ON_LAST, preferred_element_type=F32)
            return carry

        lax.fori_loop(0, FORWARD_PARTS, body, 0)

    for copy in smalls[3:]:
        copy.wait()
    center = center_s[0]
    inv = 1.0 / jnp.full((nv, width), half_s[0], F32)

    for step in range(2):
        if step == 0:
            tab_copy.wait()
        else:
            send_vectors(step)
        transposed_products(step)
        send_products(step)
        for g, copy, wanted in vector_hands(step):
            await_vectors(step, g)
            pl.when(wanted)(copy.start)
        for g in (1, 3):
            await_vectors(step, g)
        forward(step)
        pl.when(core == 0)(lambda: await_share(step, 2))
        scales = []
        for i in range(2):
            pl.when(exists(SPAN - 2 * i))(product_copy(step, i).wait_recv)
        for i in range(2):
            power = landed[step, i, rows].astype(jnp.int32).astype(F32)
            scales.append(jnp.exp2(power) * (1.0 / TOP))
        for r in range(rows):
            cut = slice(r * width, (r + 1) * width)
            v = ahead[r] + slot_sum(own + r) + shared[step, 2, r]
            for i in range(2):
                v = v + landed[step, i, r].astype(jnp.int32).astype(F32) * scales[i]
            (out1, out2)[step][:, cut] = v
            if step == 0:
                first = (v - center * win0[own + r].astype(F32)) * inv
                win1[own + r] = first.astype(jnp.bfloat16)

    for step in range(2):
        for wanted, copy in vector_sends(step):
            pl.when(wanted)(copy.wait_send)
        for g, copy, wanted in vector_hands(step):
            pl.when(wanted)(copy.wait_send)
        for i in range(2):
            share_copy(step, i).wait_send()
            pl.when(exists(2 * i - SPAN))(product_copy(step, i).wait_send)


def per_device(n, matrix_tiles, columns, vectors, center, halfwidth):
    rows, kt, width, _ = matrix_tiles.shape
    nv = vectors.shape[0]
    hbm = pl.BlockSpec(memory_space=pltpu.HBM)
    vmem = pl.BlockSpec(memory_space=pltpu.VMEM)
    out = jax.ShapeDtypeStruct(vectors.shape, F32)
    chain = rows // CHAINS * kt
    pinned = [
        pltpu.with_memory_space_constraint(a, pltpu.HBM)
        for a in (matrix_tiles, columns, vectors)
    ]
    one, two = pl.pallas_call(
        functools.partial(kernel, n),
        out_shape=(out, out),
        in_specs=[hbm] * 3 + [pl.BlockSpec(memory_space=pl.ANY)] * 2,
        out_specs=(vmem, vmem),
        scratch_shapes=[
            pltpu.VMEM(columns.shape, jnp.int32),
            pltpu.SMEM(columns.shape, jnp.int32),
            pltpu.VMEM(vectors.shape, jnp.bfloat16),
            pltpu.SMEM((1,), F32),
            pltpu.SMEM((1,), F32),
            pltpu.VMEM(matrix_tiles.shape, jnp.bfloat16),
            pltpu.VMEM(((SPAN + 1) * rows, nv, width), jnp.bfloat16),
            pltpu.VMEM(((SPAN + 1) * rows, nv, width), jnp.bfloat16),
            [pltpu.VMEM((chain + 1, nv, width), F32)] * CHAINS,
            pltpu.VMEM((rows, nv, width), F32),
            pltpu.VMEM((rows, nv, width), F32),
            pltpu.VMEM((2, 2, rows, nv, width), F32),
            pltpu.VMEM((2, 3, rows, nv, width), F32),
            pltpu.VMEM((2, 2, rows + 1, nv, width), jnp.int16),
            pltpu.VMEM((2, 2, rows + 1, nv, width), jnp.int16),
            pltpu.VMEM((SLOT_ROW + rows, 128), jnp.int32),
            pltpu.SMEM((SLOT_ROW + rows, 128), jnp.int32),
            pltpu.SemaphoreType.DMA((rows,)),
            pltpu.SemaphoreType.DMA((5,)),
            pltpu.SemaphoreType.DMA,
            pltpu.SemaphoreType.DMA((2, SPAN + 1)),
            pltpu.SemaphoreType.DMA((2, SPAN)),
            pltpu.SemaphoreType.DMA((2, 2)),
            pltpu.SemaphoreType.DMA((2, 3)),
            pltpu.SemaphoreType.DMA((2, 2)),
            pltpu.SemaphoreType.DMA((2, 2)),
        ],
        compiler_params=pltpu.CompilerParams(
            collective_id=0, has_side_effects=True, vmem_limit_bytes=32 << 20
        ),
    )(*pinned, center, halfwidth)
    initial = vectors.astype(F32)
    first = (one - center[0] * initial) / halfwidth[0]
    second = 2.0 * (two - center[0] * first) / halfwidth[0] - initial
    return first, second


def solution(mesh):
    placed = (P("tri", None, None, None), P("tri", None), P(None, "tri"), P(), P())
    return jax.shard_map(
        functools.partial(per_device, mesh.shape["tri"]),
        mesh=mesh,
        in_specs=placed,
        out_specs=(P(None, "tri"), P(None, "tri")),
        check_vma=False,
    )
```

time: 52.3 us -> 35.4 us (0.68)
  the two profiles are of different devices: /device:TPU:33 before, /device:TPU:25 now
where the time goes in v2:
time: 35.4 us; the launch traced here: 35.2 us
  Pallas kernels  32.5 us (92%)
  between operations  1.98 us (6%)
  other arithmetic  0.74 us (2%)
    pallas_call x1, Pallas kernels, per_device(): pl.pallas_call(functools.partial(kernel, n), out_shape=(out, out), in_spe...  32.5 us
    sub x1, other arithmetic, per_device(): second = 2.0 * (two - center[0] * first) / halfwidth[0] - initial  0.74 us

profile of v2, /device:TPU:25, one launch (start us, length us, event | category | flops | bytes accessed | tf_op | source)
XLA Modules:
  0.0 35.2 jit_solution(17686293456049715136)
XLA Ops:
  0.6 0.0 copy-start
  2.0 32.5 %shard_map.68 = (f32[16,2048]{1,0:T(8,128)S(1)}, f32[16,2048]{1,0:T(8,128)S(1)}) custom-call(bf16[16,12,128,128]{3,2,1,0:T(8,128)(2,1)} %tiles_hbm.1, s32[16,12]{1,0:T(8,128)} %cols_hbm.1, bf16[16,2048]{1,0:T(8,128)(2,1)} %vec_hbm.1, f32[1]{0:T(128)} %copy.7.center_hbm, f32[1]{0:T(128)} %copy.8.half_hbm), custom_call_target="tpu_custom_call" | custom-call | tf_op jit(solution)/shard_map/pallas_call | solution.py:338
  34.5 0.0 copy-done
  34.5 0.7 %convert_subtract_fusion = (f32[16,2048]{1,0:T(8,128)}, f32[16,2048]{1,0:T(8,128)}) fusion(bf16[16,2048]{1,0:T(8,128)(2,1)S(1)} %copy-done, f32[16,2048]{1,0:T(8,128)S(1)} %get-tuple-element.5, f32[]{:T(128)} %bitcast.3, f32[]{:T(128)} %bitcast.2, f32[16,2048]{1,0:T(8,128)S(1)} %get-tuple-element.4), kind=kLoop, calls=%fused_computation | loop fusion | flops 294912 | bytes 589832 | tf_op jit(solution)/shard_map/sub | solution.py:377
Async XLA Ops:
  0.6 33.9 %copy-start = (bf16[16,2048]{1,0:T(8,128)(2,1)S(1)}, bf16[16,2048]{1,0:T(8,128)(2,1)}, u32[]{:S(2)}) copy-start(bf16[16,2048]{1,0:T(8,128)(2,1)} %vec_hbm.1) | copy-start | bytes 196612

commit v3 on v2

--- a/solution.py
+++ b/solution.py
@@ -16,7 +16,6 @@
 F32 = jnp.float32
 LAST_ROW = 16
 SLOT_ROW = LAST_ROW + 8 * CHAINS
-ON_LAST = (((1,), (1,)), ((), ()))
 
 
 def kernel(
@@ -28,17 +27,20 @@
     half_hbm,
     out1,
     out2,
+    shift,
     cols_v,
     cols_s,
-    vec_v,
     center_s,
     half_s,
     tiles,
+    turned,
     win0,
     win1,
+    blocks,
     sums,
     ahead,
     total,
+    first,
     staged,
     shared,
     coded,
@@ -56,7 +58,7 @@
     precv,
 ):
     rows, kt, width, _ = tiles.shape
-    nv = vec_v.shape[0]
+    nv, span = vec_hbm.shape
     half = rows // CHAINS
     none = half * kt
     me = lax.axis_index("tri")
@@ -77,29 +79,30 @@
     smalls = [
         small(0, cols_hbm, cols_s),
         small(1, cols_hbm, cols_v),
-        small(2, vec_hbm, vec_v),
+        small(2, vec_hbm, win0.at[:, pl.ds(SPAN * span, span)]),
         small(3, center_hbm, center_s),
         small(4, half_hbm, half_s),
     ]
+
+    barrier = pltpu.get_barrier_semaphore()
+    pl.semaphore_signal(barrier, inc=1, device_id=(other,), device_id_type=MESH)
+    for d in (2, -2, 4, -4):
+
+        @pl.when(exists(d))
+        def _():
+            pl.semaphore_signal(barrier, inc=1, device_id=(me + d,), device_id_type=MESH)
+
     for copy in smalls:
         copy.start()
     for j in range(half):
         for c in range(CHAINS):
             load(c * half + j).start()
-
-    barrier = pltpu.get_barrier_semaphore()
-    pl.semaphore_signal(barrier, inc=1, device_id=(other,), device_id_type=MESH)
-    for d in (2, -2, 4, -4):
-
-        @pl.when(exists(d))
-        def _():
-            pl.semaphore_signal(barrier, inc=1, device_id=(me + d,), device_id_type=MESH)
-
     own = SPAN * rows
     win = (win0, win1)
-    smalls[2].wait()
-    for r in range(rows):
-        win0[own + r] = vec_v[:, r * width : (r + 1) * width]
+
+    def block(s):
+        return pl.ds(pl.multiple_of(s * width, width), width)
+
     for i, d in enumerate((4, 2)):
 
         @pl.when(jnp.logical_not(exists(d)))
@@ -110,13 +113,12 @@
     for step in range(2):
         shared[step, 2 * core] = jnp.zeros(shared.shape[2:], F32)
 
-    greeted = 1 + jnp.minimum(me // 2, 2) + jnp.minimum((n - 1 - me) // 2, 2)
-    pl.semaphore_wait(barrier, greeted)
 
     def vector_copy(step, i, src, dst, to):
+        from_hbm = step == 0 and src == SPAN
         return pltpu.make_async_remote_copy(
-            src_ref=win[step].at[pl.ds(src * rows, rows)],
-            dst_ref=win[step].at[pl.ds(dst * rows, rows)],
+            src_ref=vec_hbm if from_hbm else win[step].at[:, pl.ds(src * span, span)],
+            dst_ref=win[step].at[:, pl.ds(pl.multiple_of(dst * span, span), span)],
             send_sem=xsend.at[step, i],
             recv_sem=xrecv.at[step, dst],
             device_id=(to,),
@@ -124,10 +126,12 @@
         )
 
     def vector_sends(step):
+        far = vector_copy(step, 1, SPAN, SPAN - 4, me + 4)
         return [
             (core == 0, vector_copy(step, 0, SPAN, SPAN - 1, other)),
-            (exists(4), vector_copy(step, 1, SPAN, SPAN - 4, me + 4)),
+            (exists(4) & (core == 1), far),
             (exists(2), vector_copy(step, 2, SPAN, SPAN - 2, me + 2)),
+            (exists(4) & (core == 0), far),
         ]
 
     def vector_hands(step):
@@ -144,8 +148,6 @@
     def send_vectors(step):
         for wanted, copy in vector_sends(step):
             pl.when(wanted)(copy.start)
-
-    send_vectors(0)
 
     for c in range(CHAINS):
         sums[c][none] = jnp.zeros((nv, width), F32)
@@ -227,7 +229,7 @@
     def add_pair(step, c, j, k):
         r = c * half + j
         pair = jnp.concatenate([tiles[r, k], tiles[r, k + 1]], axis=1)
-        both = jnp.dot(win[step][own + r], pair, preferred_element_type=F32)
+        both = jnp.dot(win[step][:, block(own + r)], pair, preferred_element_type=F32)
         for i in range(2):
             slot = tab_s[SLOT_ROW + r, k + i]
             weight = jnp.where(slot == own + r, 0.5, 1.0).astype(F32)
@@ -238,10 +240,13 @@
     def slot_sum(s):
         return sum(sums[c][tab_s[LAST_ROW + 8 * c, s]] for c in range(CHAINS))
 
-    def send_products(step):
+    def stage_products(step):
         for i in range(2):
             for r in range(rows):
                 staged[step, i, r] = slot_sum((2 * i + 1) * rows + r)
+
+    def send_products(step):
+        for i in range(2):
             share_copy(step, i).start()
         for i in range(2):
             if i == 0:
@@ -263,18 +268,28 @@
             coded[step, i, rows] = power.astype(jnp.int32).astype(jnp.int16)
             pl.when(exists(2 * i - SPAN))(product_copy(step, i).start)
 
+    def turn():
+        def body(r, carry):
+            for k in range(kt):
+                turned[r, k * width : (k + 1) * width, :] = tiles[r, k].T
+            return carry
+
+        lax.fori_loop(0, rows, body, 0)
+
     def forward(step):
+        for s in range(own + rows):
+            blocks[s] = win[step][:, block(s)]
+
         def body(part, carry):
             for i in range(rows // FORWARD_PARTS):
                 r = part * (rows // FORWARD_PARTS) + i
                 picked = []
                 for k in range(kt):
-                    s = tab_s[SLOT_ROW + r, k]
-                    weight = jnp.full((nv, width), jnp.where(s == own + r, 0.5, 1.0), F32)
-                    picked.append(win[step][s] * weight.astype(jnp.bfloat16))
+                    slot = tab_s[SLOT_ROW + r, k]
+                    weight = jnp.full((nv, width), jnp.where(slot == own + r, 0.5, 1.0), F32)
+                    picked.append(blocks[slot] * weight.astype(jnp.bfloat16))
                 x = jnp.concatenate(picked, axis=1)
-                w = jnp.concatenate([tiles[r, k] for k in range(kt)], axis=1)
-                ahead[r] = lax.dot_general(x, w, ON_LAST, preferred_element_type=F32)
+                ahead[r] = jnp.dot(x, turned[r], preferred_element_type=F32)
             return carry
 
         lax.fori_loop(0, FORWARD_PARTS, body, 0)
@@ -284,13 +299,23 @@
     center = center_s[0]
     inv = 1.0 / jnp.full((nv, width), half_s[0], F32)
 
+    shift[...] = jnp.broadcast_to((center * inv)[:1, :1], shift.shape)
+
+    greeted = 1 + jnp.minimum(me // 2, 2) + jnp.minimum((n - 1 - me) // 2, 2)
     for step in range(2):
         if step == 0:
             tab_copy.wait()
+            smalls[2].wait()
         else:
             send_vectors(step)
         transposed_products(step)
+        stage_products(step)
+        if step == 0:
+            pl.semaphore_wait(barrier, greeted)
+            send_vectors(step)
         send_products(step)
+        if step == 0:
+            turn()
         for g, copy, wanted in vector_hands(step):
             await_vectors(step, g)
             pl.when(wanted)(copy.start)
@@ -309,10 +334,12 @@
             v = ahead[r] + slot_sum(own + r) + shared[step, 2, r]
             for i in range(2):
                 v = v + landed[step, i, r].astype(jnp.int32).astype(F32) * scales[i]
-            (out1, out2)[step][:, cut] = v
             if step == 0:
-                first = (v - center * win0[own + r].astype(F32)) * inv
-                win1[own + r] = first.astype(jnp.bfloat16)
+                out1[:, cut] = v * inv
+                first[r] = v * inv - win0[:, block(own + r)].astype(F32) * (center * inv)
+                win1[:, block(own + r)] = first[r].astype(jnp.bfloat16)
+            else:
+                out2[:, cut] = 2.0 * (v - center * first[r]) * inv
 
     for step in range(2):
         for wanted, copy in vector_sends(step):
@@ -335,21 +362,23 @@
         pltpu.with_memory_space_constraint(a, pltpu.HBM)
         for a in (matrix_tiles, columns, vectors)
     ]
-    one, two = pl.pallas_call(
+    one, two, shift = pl.pallas_call(
         functools.partial(kernel, n),
-        out_shape=(out, out),
+        out_shape=(out, out, jax.ShapeDtypeStruct((1, vectors.shape[1]), F32)),
         in_specs=[hbm] * 3 + [pl.BlockSpec(memory_space=pl.ANY)] * 2,
-        out_specs=(vmem, vmem),
+        out_specs=(vmem, vmem, vmem),
         scratch_shapes=[
             pltpu.VMEM(columns.shape, jnp.int32),
             pltpu.SMEM(columns.shape, jnp.int32),
-            pltpu.VMEM(vectors.shape, jnp.bfloat16),
             pltpu.SMEM((1,), F32),
             pltpu.SMEM((1,), F32),
             pltpu.VMEM(matrix_tiles.shape, jnp.bfloat16),
-            pltpu.VMEM(((SPAN + 1) * rows, nv, width), jnp.bfloat16),
+            pltpu.VMEM((rows, kt * width, width), jnp.bfloat16),
+            pltpu.VMEM((nv, (SPAN + 1) * vectors.shape[1]), jnp.bfloat16),
+            pltpu.VMEM((nv, (SPAN + 1) * vectors.shape[1]), jnp.bfloat16),
             pltpu.VMEM(((SPAN + 1) * rows, nv, width), jnp.bfloat16),
             [pltpu.VMEM((chain + 1, nv, width), F32)] * CHAINS,
+            pltpu.VMEM((rows, nv, width), F32),
             pltpu.VMEM((rows, nv, width), F32),
             pltpu.VMEM((rows, nv, width), F32),
             pltpu.VMEM((2, 2, rows, nv, width), F32),
@@ -373,9 +402,7 @@
         ),
     )(*pinned, center, halfwidth)
     initial = vectors.astype(F32)
-    first = (one - center[0] * initial) / halfwidth[0]
-    second = 2.0 * (two - center[0] * first) / halfwidth[0] - initial
-    return first, second
+    return one - initial * shift, two - initial
 
 
 def solution(mesh):

time: 35.4 us -> 31.3 us (0.88); the launches traced: 35.2 us -> 30.8 us
  Pallas kernels: 32.5 us -> 28 us
    pallas_call x1, Pallas kernels: 32.5 us -> 28 us  [per_device(): pl.pallas_call(functools.partial(kernel, n), out_shape=(out, out, jax.Sha...]
where the time goes in v3:
time: 31.3 us; the launch traced here: 30.8 us
  Pallas kernels  28 us (89%)
  between operations  1.98 us (6%)
  other arithmetic  0.73 us (2%)
    pallas_call x1, Pallas kernels, per_device(): pl.pallas_call(functools.partial(kernel, n), out_shape=(out, out, jax.Sha...  28 us
    sub x1, other arithmetic, per_device(): return (one - initial * shift, two - initial)  0.73 us

profile of v3, /device:TPU:25, one launch (start us, length us, event | category | flops | bytes accessed | tf_op | source)
XLA Modules:
  0.0 30.8 jit_solution(13787970396342819936)
XLA Ops:
  0.6 0.0 copy-start
  2.0 28.0 %shard_map.68 = (f32[16,2048]{1,0:T(8,128)S(1)}, f32[16,2048]{1,0:T(8,128)S(1)}, f32[1,2048]{1,0:T(1,128)S(1)}) custom-call(bf16[16,12,128,128]{3,2,1,0:T(8,128)(2,1)} %tiles_hbm.1, s32[16,12]{1,0:T(8,128)} %cols_hbm.1, bf16[16,2048]{1,0:T(8,128)(2,1)} %vec_hbm.1, f32[1]{0:T(128)S(6)} %copy.7.center_hbm, f32[1]{0:T(128)S(6)} %copy.8.half_hbm), custom_call_target="tpu_custom_call" | custom-call | tf_op jit(solution)/shard_map/pallas_call | solution.py:365
  30.0 0.0 copy-done
  30.0 0.7 %convert_subtract_fusion = (f32[16,2048]{1,0:T(8,128)}, f32[16,2048]{1,0:T(8,128)}) fusion(f32[16,2048]{1,0:T(8,128)S(1)} %get-tuple-element.7, bf16[16,2048]{1,0:T(8,128)(2,1)S(1)} %copy-done, f32[16,2048]{1,0:T(8,128)S(1)} %get-tuple-element.5, f32[2048]{0:T(1024)S(1)} %bitcast.1), kind=kLoop, calls=%fused_computation | loop fusion | flops 131072 | bytes 598016 | tf_op jit(solution)/shard_map/sub | solution.py:405
Async XLA Ops:
  0.6 29.4 %copy-start = (bf16[16,2048]{1,0:T(8,128)(2,1)S(1)}, bf16[16,2048]{1,0:T(8,128)(2,1)}, u32[]{:S(2)}) copy-start(bf16[16,2048]{1,0:T(8,128)(2,1)} %vec_hbm.1) | copy-start | bytes 196612

commit v4 on v3

--- a/solution.py
+++ b/solution.py
@@ -10,6 +10,7 @@
 SPAN = 4
 BEHIND_PARTS = 2
 FORWARD_PARTS = 2
+LINE = 8
 CHAINS = 2
 TOP = 32766.0
 MESH = pl.DeviceIdType.MESH
@@ -45,6 +46,7 @@
     shared,
     coded,
     landed,
+    relayed,
     tab_v,
     tab_s,
     tile_sem,
@@ -56,19 +58,26 @@
     srecv,
     psend,
     precv,
+    rrecv,
 ):
     rows, kt, width, _ = tiles.shape
     nv, span = vec_hbm.shape
     half = rows // CHAINS
     none = half * kt
     me = lax.axis_index("tri")
+    chip = lax.rem(me // 2, LINE)
+
+    def exists(d):
+        return (me + d >= 0) & (me + d < n)
+
+
     core = lax.rem(me, 2)
+    relays = (chip == 1) & exists(-4)
+    gathers = (chip == 0) & exists(-2)
+    goes = (exists(-4) & (chip != 1), exists(-2))
+    comes = (exists(4) & (chip != LINE - 1), exists(2))
     other = me + 1 - 2 * core
     lowest = (me - SPAN) * rows
-
-    def exists(d):
-        return (me + d >= 0) & (me + d < n)
-
 
     def load(r):
         return pltpu.make_async_copy(tiles_hbm.at[r], tiles.at[r], tile_sem.at[r])
@@ -86,9 +95,9 @@
 
     barrier = pltpu.get_barrier_semaphore()
     pl.semaphore_signal(barrier, inc=1, device_id=(other,), device_id_type=MESH)
-    for d in (2, -2, 4, -4):
-
-        @pl.when(exists(d))
+    for d, wanted in ((2, comes[1]), (-2, exists(-2)), (4, comes[0]), (-4, exists(-4))):
+
+        @pl.when(wanted)
         def _():
             pl.semaphore_signal(barrier, inc=1, device_id=(me + d,), device_id_type=MESH)
 
@@ -103,12 +112,16 @@
     def block(s):
         return pl.ds(pl.multiple_of(s * width, width), width)
 
-    for i, d in enumerate((4, 2)):
-
-        @pl.when(jnp.logical_not(exists(d)))
+    for i in range(2):
+
+        @pl.when(jnp.logical_not(comes[i]))
         def _():
             for step in range(2):
                 landed[step, i] = jnp.zeros(landed.shape[2:], landed.dtype)
+
+    @pl.when(jnp.logical_not(gathers))
+    def _():
+        relayed[...] = jnp.zeros(relayed.shape, relayed.dtype)
 
     for step in range(2):
         shared[step, 2 * core] = jnp.zeros(shared.shape[2:], F32)
@@ -125,13 +138,15 @@
             device_id_type=MESH,
         )
 
+    far_first = jnp.where(chip >= LINE - 2, chip == LINE - 2, core == 1)
+
     def vector_sends(step):
         far = vector_copy(step, 1, SPAN, SPAN - 4, me + 4)
         return [
             (core == 0, vector_copy(step, 0, SPAN, SPAN - 1, other)),
-            (exists(4) & (core == 1), far),
+            (exists(4) & far_first, far),
             (exists(2), vector_copy(step, 2, SPAN, SPAN - 2, me + 2)),
-            (exists(4) & (core == 0), far),
+            (exists(4) & jnp.logical_not(far_first), far),
         ]
 
     def vector_hands(step):
@@ -212,6 +227,16 @@
             device_id_type=MESH,
         )
 
+    def relay_copy(step):
+        return pltpu.make_async_remote_copy(
+            src_ref=coded.at[step, 0],
+            dst_ref=relayed.at[step],
+            send_sem=psend.at[step, 0],
+            recv_sem=rrecv.at[step],
+            device_id=(me - 2,),
+            device_id_type=MESH,
+        )
+
     def transposed_products(step):
         def body(part, carry):
             for i in range(half // BEHIND_PARTS):
@@ -253,9 +278,14 @@
                 pl.when(core == 1)(lambda: await_share(step, 0))
             else:
                 await_share(step, 1)
+                pl.when(gathers)(relay_copy(step).wait_recv)
+                power = relayed[step, rows].astype(jnp.int32).astype(F32)
+                unit = jnp.exp2(power) * (1.0 / TOP)
             most = jnp.zeros((nv, width), F32)
             for r in range(rows):
                 v = slot_sum(2 * i * rows + r) + shared[step, i, r]
+                if i == 1:
+                    v = v + relayed[step, r].astype(jnp.int32).astype(F32) * unit
                 total[r] = v
                 most = jnp.maximum(most, jnp.abs(v))
             peak = jnp.maximum(jnp.max(most, axis=1, keepdims=True), 1e-30)
@@ -266,7 +296,9 @@
                     jnp.round(total[r] * scale).astype(jnp.int32).astype(jnp.int16)
                 )
             coded[step, i, rows] = power.astype(jnp.int32).astype(jnp.int16)
-            pl.when(exists(2 * i - SPAN))(product_copy(step, i).start)
+            pl.when(goes[i])(product_copy(step, i).start)
+            if i == 0:
+                pl.when(relays)(relay_copy(step).start)
 
     def turn():
         def body(r, carry):
@@ -302,17 +334,28 @@
     shift[...] = jnp.broadcast_to((center * inv)[:1, :1], shift.shape)
 
     greeted = 1 + jnp.minimum(me // 2, 2) + jnp.minimum((n - 1 - me) // 2, 2)
+    greeted = greeted - jnp.where(relays, 1, 0)
+    def enter():
+        pl.semaphore_wait(barrier, greeted)
+        send_vectors(0)
+
     for step in range(2):
         if step == 0:
             tab_copy.wait()
             smalls[2].wait()
+
+            @pl.when(chip >= LINE - 2)
+            def _():
+                enter()
         else:
             send_vectors(step)
         transposed_products(step)
         stage_products(step)
         if step == 0:
-            pl.semaphore_wait(barrier, greeted)
-            send_vectors(step)
+
+            @pl.when(chip < LINE - 2)
+            def _():
+                enter()
         send_products(step)
         if step == 0:
             turn()
@@ -325,7 +368,7 @@
         pl.when(core == 0)(lambda: await_share(step, 2))
         scales = []
         for i in range(2):
-            pl.when(exists(SPAN - 2 * i))(product_copy(step, i).wait_recv)
+            pl.when(comes[i])(product_copy(step, i).wait_recv)
         for i in range(2):
             power = landed[step, i, rows].astype(jnp.int32).astype(F32)
             scales.append(jnp.exp2(power) * (1.0 / TOP))
@@ -348,7 +391,8 @@
             pl.when(wanted)(copy.wait_send)
         for i in range(2):
             share_copy(step, i).wait_send()
-            pl.when(exists(2 * i - SPAN))(product_copy(step, i).wait_send)
+            pl.when(goes[i])(product_copy(step, i).wait_send)
+        pl.when(relays)(relay_copy(step).wait_send)
 
 
 def per_device(n, matrix_tiles, columns, vectors, center, halfwidth):
@@ -385,6 +429,7 @@
             pltpu.VMEM((2, 3, rows, nv, width), F32),
             pltpu.VMEM((2, 2, rows + 1, nv, width), jnp.int16),
             pltpu.VMEM((2, 2, rows + 1, nv, width), jnp.int16),
+            pltpu.VMEM((2, rows + 1, nv, width), jnp.int16),
             pltpu.VMEM((SLOT_ROW + rows, 128), jnp.int32),
             pltpu.SMEM((SLOT_ROW + rows, 128), jnp.int32),
             pltpu.SemaphoreType.DMA((rows,)),
@@ -396,6 +441,7 @@
             pltpu.SemaphoreType.DMA((2, 3)),
             pltpu.SemaphoreType.DMA((2, 2)),
             pltpu.SemaphoreType.DMA((2, 2)),
+            pltpu.SemaphoreType.DMA((2,)),
         ],
         compiler_params=pltpu.CompilerParams(
             collective_id=0, has_side_effects=True, vmem_limit_bytes=32 << 20

time: 31.3 us -> 30.8 us (0.984)
  Pallas kernels: 28 us -> 27.6 us
    pallas_call x1, Pallas kernels: 28 us -> 27.6 us  [per_device(): pl.pallas_call(functools.partial(kernel, n), out_shape=(out, out, jax.Sha...]
where the time goes in v4:
time: 30.8 us; the launch traced here: 30.4 us
  Pallas kernels  27.6 us (90%)
  between operations  1.98 us (6%)
  other arithmetic  0.73 us (2%)
    pallas_call x1, Pallas kernels, per_device(): pl.pallas_call(functools.partial(kernel, n), out_shape=(out, out, jax.Sha...  27.6 us
    sub x1, other arithmetic, per_device(): return (one - initial * shift, two - initial)  0.73 us

profile of v4, /device:TPU:25, one launch (start us, length us, event | category | flops | bytes accessed | tf_op | source)
XLA Modules:
  0.0 30.4 jit_solution(10860391099711129056)
XLA Ops:
  0.6 0.0 copy-start
  2.0 27.6 %shard_map.68 = (f32[16,2048]{1,0:T(8,128)S(1)}, f32[16,2048]{1,0:T(8,128)S(1)}, f32[1,2048]{1,0:T(1,128)S(1)}) custom-call(bf16[16,12,128,128]{3,2,1,0:T(8,128)(2,1)} %tiles_hbm.1, s32[16,12]{1,0:T(8,128)} %cols_hbm.1, bf16[16,2048]{1,0:T(8,128)(2,1)} %vec_hbm.1, f32[1]{0:T(128)S(6)} %copy.7.center_hbm, f32[1]{0:T(128)S(6)} %copy.8.half_hbm), custom_call_target="tpu_custom_call" | custom-call | tf_op jit(solution)/shard_map/pallas_call | solution.py:409
  29.6 0.0 copy-done
  29.6 0.7 %convert_subtract_fusion = (f32[16,2048]{1,0:T(8,128)}, f32[16,2048]{1,0:T(8,128)}) fusion(f32[16,2048]{1,0:T(8,128)S(1)} %get-tuple-element.7, bf16[16,2048]{1,0:T(8,128)(2,1)S(1)} %copy-done, f32[16,2048]{1,0:T(8,128)S(1)} %get-tuple-element.5, f32[2048]{0:T(1024)S(1)} %bitcast.1), kind=kLoop, calls=%fused_computation | loop fusion | flops 131072 | bytes 598016 | tf_op jit(solution)/shard_map/sub | solution.py:451
Async XLA Ops:
  0.6 29.0 %copy-start = (bf16[16,2048]{1,0:T(8,128)(2,1)S(1)}, bf16[16,2048]{1,0:T(8,128)(2,1)}, u32[]{:S(2)}) copy-start(bf16[16,2048]{1,0:T(8,128)(2,1)} %vec_hbm.1) | copy-start | bytes 196612

commit v5 on v4

--- a/solution.py
+++ b/solution.py
@@ -273,6 +273,8 @@
     def send_products(step):
         for i in range(2):
             share_copy(step, i).start()
+        if step == 0:
+            pl.when(chip < LINE - 2)(lambda: send_vectors(0))
         for i in range(2):
             if i == 0:
                 pl.when(core == 1)(lambda: await_share(step, 0))
@@ -355,7 +357,7 @@
 
             @pl.when(chip < LINE - 2)
             def _():
-                enter()
+                pl.semaphore_wait(barrier, greeted)
         send_products(step)
         if step == 0:
             turn()

time: 30.8 us -> 30.7 us (level)
  no operation moved by 1% of the time
where the time goes in v5:
time: 30.7 us; the launch traced here: 30.2 us
  Pallas kernels  27.4 us (89%)
  between operations  1.98 us (6%)
  other arithmetic  0.73 us (2%)
    pallas_call x1, Pallas kernels, per_device(): pl.pallas_call(functools.partial(kernel, n), out_shape=(out, out, jax.Sha...  27.4 us
    sub x1, other arithmetic, per_device(): return (one - initial * shift, two - initial)  0.73 us

profile of v5, /device:TPU:25, one launch (start us, length us, event | category | flops | bytes accessed | tf_op | source)
XLA Modules:
  0.0 30.2 jit_solution(2118525656296019247)
XLA Ops:
  0.6 0.0 copy-start
  2.0 27.4 %shard_map.68 = (f32[16,2048]{1,0:T(8,128)S(1)}, f32[16,2048]{1,0:T(8,128)S(1)}, f32[1,2048]{1,0:T(1,128)S(1)}) custom-call(bf16[16,12,128,128]{3,2,1,0:T(8,128)(2,1)} %tiles_hbm.1, s32[16,12]{1,0:T(8,128)} %cols_hbm.1, bf16[16,2048]{1,0:T(8,128)(2,1)} %vec_hbm.1, f32[1]{0:T(128)S(6)} %copy.7.center_hbm, f32[1]{0:T(128)S(6)} %copy.8.half_hbm), custom_call_target="tpu_custom_call" | custom-call | tf_op jit(solution)/shard_map/pallas_call | solution.py:411
  29.4 0.0 copy-done
  29.4 0.7 %convert_subtract_fusion = (f32[16,2048]{1,0:T(8,128)}, f32[16,2048]{1,0:T(8,128)}) fusion(f32[16,2048]{1,0:T(8,128)S(1)} %get-tuple-element.7, bf16[16,2048]{1,0:T(8,128)(2,1)S(1)} %copy-done, f32[16,2048]{1,0:T(8,128)S(1)} %get-tuple-element.5, f32[2048]{0:T(1024)S(1)} %bitcast.1), kind=kLoop, calls=%fused_computation | loop fusion | flops 131072 | bytes 598016 | tf_op jit(solution)/shard_map/sub | solution.py:453
Async XLA Ops:
  0.6 28.8 %copy-start = (bf16[16,2048]{1,0:T(8,128)(2,1)S(1)}, bf16[16,2048]{1,0:T(8,128)(2,1)}, u32[]{:S(2)}) copy-start(bf16[16,2048]{1,0:T(8,128)(2,1)} %vec_hbm.1) | copy-start | bytes 196612
